TPU v7x, 512 devices: a whole 4x4x16 slice. The times are simulated.
512 devices in a mesh: aux: 64 (over y, z), occ: 8 (over x, core).
Axes of the slice: x: 4, y: 4, z: 16, core: 2. Of those that a mesh axis runs over, the one named last changes fastest.
Arguments:
- factor_tiles: bfloat16 [128, 24, 4, 128, 128], P('aux'), may hold values from -1 to 1
- tile_cols: int32 [128, 24, 4], P('aux'), may hold values from 0 to 23, as said below
- coeffs: bfloat16 [3072, 256], P(None, 'occ'), may hold values from -0.25 to 0.25
- pair_owner: int32 [576], P('aux'), may hold values from 0 to 575, each once
Outputs:
- exchange_tiles: float32 [576, 128, 128], P('aux', 'occ')
Inputs may be any that keep to these rules, and one draw needn't show every extreme that they name: `tile_cols`: for each auxiliary function and basis block row, the 4 listed column blocks are distinct. `pair_owner`: each basis block pair appears exactly once.
All inputs are finite; a program needn't handle non-finite values.
Results may differ from a plain program's by a relative error of at most 0.0015.
Values may be sent and summed in bfloat16 or wider, within the bound.
A program may use at most 128 MiB of HBM per device.

v0:
```python
import jax
import jax.numpy as jnp
from jax import lax
from jax.sharding import PartitionSpec as P


def shards(factor_tiles, tile_cols, coeffs, pair_owner):
    aux_count = factor_tiles.shape[0]
    block_count = factor_tiles.shape[1]
    tile_width = factor_tiles.shape[3]
    local_occ = coeffs.shape[1]
    blocks = coeffs.reshape(block_count, tile_width, local_occ)
    picked = blocks[tile_cols]
    halves = jnp.einsum(
        "qmsrl,qmsli->mrqi", factor_tiles, picked, preferred_element_type=jnp.float32
    ).astype(jnp.bfloat16)
    halves = halves.reshape(block_count, tile_width, aux_count * local_occ)
    row_blocks = pair_owner // block_count
    col_blocks = pair_owner % block_count
    gathered = lax.all_gather(halves, "aux", axis=2, tiled=True)
    row_part = jnp.take(gathered, row_blocks, axis=0)
    col_part = jnp.take(gathered, col_blocks, axis=0)
    partial_tiles = jnp.einsum(
        "sbw,scw->sbc", row_part, col_part, preferred_element_type=jnp.float32
    )
    summed = lax.psum(partial_tiles, "occ")
    share_rows = tile_width // lax.axis_size("occ")
    return lax.dynamic_slice_in_dim(summed, lax.axis_index("occ") * share_rows, share_rows, 1)


def solution(mesh):
    placed = (P("aux", None, None, None, None), P("aux", None, None), P(None, "occ"), P("aux"))
    return jax.shard_map(
        shards, mesh=mesh, in_specs=placed, out_specs=P("aux", "occ", None), check_vma=False
    )
```

profile of v0, /device:TPU:8, one launch (start us, length us, event | category | flops | bytes accessed | tf_op | source)
XLA Modules:
  0.0 413.8 jit_solution(6229224219525203429)
XLA Ops:
  6.5 0.0 copy-start
  6.5 0.0 all-gather.2.cloned.1.call-start
  6.5 0.9 copy-done
  7.5 0.7 compare_select_fusion
  8.2 0.1 copy.15
  8.3 0.1 reshape.31
  8.4 0.0 copy-start.2
  8.4 0.9 gather_fusion
  9.3 5.0 %fusion.14 = bf16[24,2,32,128]{3,2,1,0:T(8,128)(2,1)S(1)} fusion(bf16[2,24,4,128,128]{4,3,2,1,0:T(8,128)(2,1)} %param.6, bf16[2,24,4,128,32]{3,4,2,1,0:T(8,128)(2,1)S(1)} %bitcast.14), kind=kOutput, calls=%fused_computation.13 | convolution fusion | flops 201523200 | bytes 8257536 | tf_op jit(solution)/shard_map/qmsrl,qmsli->mrqi/dot_general | solution.py:14
  14.3 1.0 copy.19
  15.3 0.0 all-gather.2.cloned.1.call-update
  15.3 0.0 all-reduce.2.cloned.1.call-start
  15.4 0.0 copy-done.2
  15.4 247.6 %all-gather.2.cloned.1.call-done = bf16[24,128,4096]{1,0,2:T(8,128)(2,1)} async-done(((bf16[24,128,64]{1,0,2:T(8,128)(2,1)}), bf16[24,128,4096]{1,0,2:T(8,128)(2,1)}) %all-gather.2.cloned.1.call-update) | async-done | bytes 25165840 | tf_op jit(solution)/shard_map/all_gather | solution.py:20
  263.0 31.6 %copy.20 = bf16[24,128,4096]{2,1,0:T(8,128)(2,1)} copy(bf16[24,128,4096]{1,0,2:T(8,128)(2,1)} %all-gather.2.cloned.1.call-done) | data formatting | bytes 50331648 | tf_op jit(solution)/shard_map/all_gather | solution.py:20
  294.6 13.2 %gather_fusion.2 = bf16[9,128,4096]{2,1,0:T(8,128)(2,1)} fusion(bf16[24,128,4096]{2,1,0:T(8,128)(2,1)} %copy.20, s32[1024]{0:T(1024)S(1)} %get-tuple-element.12), kind=kCustom, calls=%fused_computation.1.clone | custom fusion | bytes 18874404 | tf_op jit(solution)/shard_map/jit(_take)/gather | solution.py:22
  307.8 13.3 %gather_fusion.1 = bf16[9,128,4096]{2,1,0:T(8,128)(2,1)} fusion(bf16[24,128,4096]{2,1,0:T(8,128)(2,1)} %copy.20, s32[1024]{0:T(1024)S(1)} %get-tuple-element.13), kind=kCustom, calls=%fused_computation.clone | custom fusion | bytes 18874404 | tf_op jit(solution)/shard_map/jit(_take)/gather | solution.py:21
  321.1 0.0 copy-start.1
  321.1 10.0 %fusion = f32[9,128,128]{2,1,0:T(8,128)} fusion(bf16[9,128,4096]{2,1,0:T(8,128)(2,1)} %gather_fusion.2, bf16[9,128,4096]{2,1,0:T(8,128)(2,1)} %gather_fusion.1, pred[9]{0:T(512)(128)(4,1)S(1)} %get-tuple-element.10, pred[9]{0:T(512)(128)(4,1)S(1)} %get-tuple-element.6), kind=kOutput, calls=%fused_computation.3 | convolution fusion | flops 1217396736 | bytes 19464210 | tf_op jit(solution)/shard_map/sbw,scw->sbc/dot_general | solution.py:23
  331.1 0.0 all-reduce.2.cloned.1.call-update
  331.1 74.3 %all-reduce.2.cloned.1.call-done = f32[9,128,128]{2,1,0:T(8,128)} async-done(((f32[9,128,128]{2,1,0:T(8,128)}), f32[9,128,128]{2,1,0:T(8,128)}) %all-reduce.2.cloned.1.call-update) | async-done | bytes 589840 | tf_op jit(solution)/shard_map/psum | solution.py:26
  405.4 1.5 constant_dynamic-slice_fusion
  406.9 0.0 copy-done.1
  (4 shorter events, 0.1 us)
Async XLA Ops:
  6.5 0.9 copy-start
  6.5 256.5 %all-gather.2.cloned.1.call-start = ((), (), s32[]{:S(2)}) async-start(), calls=%async_computation | async-start | bytes 25559040 | tf_op jit(solution)/shard_map/all_gather | solution.py:20
  8.4 7.0 %copy-start.2 = (s32[9]{0:T(128)S(1)}, s32[9]{0:T(128)}, u32[]{:S(2)}) copy-start(s32[9]{0:T(128)} %param.9) | copy-start | bytes 112
  15.3 390.1 %all-reduce.2.cloned.1.call-start = ((), (), s32[]{:S(2)}) async-start(), calls=%async_computation.1 | async-start | bytes 1179648 | tf_op jit(solution)/shard_map/psum | solution.py:26
  321.1 85.8 %copy-start.1 = (bf16[3072,32]{0,1:T(8,128)(2,1)S(1)}, bf16[3072,32]{0,1:T(8,128)(2,1)}, u32[]{:S(2)}) copy-start(bf16[3072,32]{0,1:T(8,128)(2,1)} %param.8) | copy-start | bytes 589828
Sparse Core Ops, SparseCore 0:
  15.4 247.5 all-gather.1
  331.3 74.0 all-reduce.1
where the time goes:
time: 415 us; the launch traced here: 414 us
  waiting for transfers between devices  322 us (78%)
  local copies, waits for them, and re-layouts  62.7 us (15%)
  matrix products  15 us (4%)
  between operations  13.5 us (3%)
    all_gather x1, waiting for transfers between devices, shards(): gathered = lax.all_gather(halves, 'aux', axis=2, tiled=True)  248 us
    psum x1, waiting for transfers between devices, shards(): summed = lax.psum(partial_tiles, 'occ')  74.3 us
    all_gather x1, local copies, waits for them, and re-layouts, shards(): gathered = lax.all_gather(halves, 'aux', axis=2, tiled=True)  31.6 us
    gather x1, local copies, waits for them, and re-layouts, shards(): row_part = jnp.take(gathered, row_blocks, axis=0)  13.3 us
    gather x1, local copies, waits for them, and re-layouts, shards(): col_part = jnp.take(gathered, col_blocks, axis=0)  13.2 us
    dot_general x1, matrix products, shards(): jnp.einsum('sbw,scw->sbc', row_part, col_part, preferred_element_type=jnp...  10 us
  transfers between devices with their start and end apart: 2, of which 2 were waited for; matrix products, arithmetic and copies ran while one was open for 0% of the time, Pallas kernels for 0%

commit v1 on v0

--- a/solution.py
+++ b/solution.py
@@ -23,7 +23,7 @@
     partial_tiles = jnp.einsum(
         "sbw,scw->sbc", row_part, col_part, preferred_element_type=jnp.float32
     )
-    summed = lax.psum(partial_tiles, "occ")
+    summed = jnp.sum(lax.all_gather(partial_tiles, "occ"), axis=0)
     share_rows = tile_width // lax.axis_size("occ")
     return lax.dynamic_slice_in_dim(summed, lax.axis_index("occ") * share_rows, share_rows, 1)
 

time: 415 us -> 383 us (0.923)
  the two profiles are of different devices: /device:TPU:8 before, /device:TPU:1 now
where the time goes in v1:
time: 383 us; the launch traced here: 382 us
  waiting for transfers between devices  289 us (75%)
  local copies, waits for them, and re-layouts  61.8 us (16%)
  matrix products  15 us (4%)
  between operations  13.5 us (4%)
    all_gather x1, waiting for transfers between devices, shards(): gathered = lax.all_gather(halves, 'aux', axis=2, tiled=True)  249 us
    all_gather x1, waiting for transfers between devices, shards(): summed = jnp.sum(lax.all_gather(partial_tiles, 'occ'), axis=0)  39.3 us
    all_gather x1, local copies, waits for them, and re-layouts, shards(): gathered = lax.all_gather(halves, 'aux', axis=2, tiled=True)  31.6 us
    gather x1, local copies, waits for them, and re-layouts, shards(): row_part = jnp.take(gathered, row_blocks, axis=0)  13.3 us
    gather x1, local copies, waits for them, and re-layouts, shards(): col_part = jnp.take(gathered, col_blocks, axis=0)  13.2 us
    dot_general x1, matrix products, shards(): jnp.einsum('sbw,scw->sbc', row_part, col_part, preferred_element_type=jnp...  10 us
  transfers between devices with their start and end apart: 2, of which 2 were waited for; matrix products, arithmetic and copies ran while one was open for 0% of the time, Pallas kernels for 0%

profile of v1, /device:TPU:1, one launch (start us, length us, event | category | flops | bytes accessed | tf_op | source)
XLA Modules:
  0.0 382.4 jit_solution(12042000740575578761)
XLA Ops:
  6.5 0.0 copy-start
  6.5 0.0 all-gather.4.cloned.1.call-start
  6.5 0.9 copy-done
  7.5 0.7 compare_select_fusion
  8.2 0.1 copy.15
  8.3 0.1 reshape.31
  8.4 0.0 copy-start.2
  8.4 0.9 gather_fusion
  9.3 5.0 %fusion.14 = bf16[24,2,32,128]{3,2,1,0:T(8,128)(2,1)S(1)} fusion(bf16[2,24,4,128,128]{4,3,2,1,0:T(8,128)(2,1)} %param.6, bf16[2,24,4,128,32]{3,4,2,1,0:T(8,128)(2,1)S(1)} %bitcast.15), kind=kOutput, calls=%fused_computation.13 | convolution fusion | flops 201523200 | bytes 8257536 | tf_op jit(solution)/shard_map/qmsrl,qmsli->mrqi/dot_general | solution.py:14
  14.3 1.0 copy.19
  15.3 0.0 all-gather.4.cloned.1.call-update
  15.3 0.0 all-gather.6.cloned.1.call-start
  15.4 0.0 copy-done.2
  15.4 249.4 %all-gather.4.cloned.1.call-done = bf16[24,128,4096]{1,0,2:T(8,128)(2,1)} async-done(((bf16[24,128,64]{1,0,2:T(8,128)(2,1)}), bf16[24,128,4096]{1,0,2:T(8,128)(2,1)}) %all-gather.4.cloned.1.call-update) | async-done | bytes 25165840 | tf_op jit(solution)/shard_map/all_gather | solution.py:20
  264.8 31.6 %copy.20 = bf16[24,128,4096]{2,1,0:T(8,128)(2,1)} copy(bf16[24,128,4096]{1,0,2:T(8,128)(2,1)} %all-gather.4.cloned.1.call-done) | data formatting | bytes 50331648 | tf_op jit(solution)/shard_map/all_gather | solution.py:20
  296.4 13.2 %gather_fusion.2 = bf16[9,128,4096]{2,1,0:T(8,128)(2,1)} fusion(bf16[24,128,4096]{2,1,0:T(8,128)(2,1)} %copy.20, s32[1024]{0:T(1024)S(1)} %get-tuple-element.12), kind=kCustom, calls=%fused_computation.1.clone | custom fusion | bytes 18874404 | tf_op jit(solution)/shard_map/jit(_take)/gather | solution.py:22
  309.6 13.3 %gather_fusion.1 = bf16[9,128,4096]{2,1,0:T(8,128)(2,1)} fusion(bf16[24,128,4096]{2,1,0:T(8,128)(2,1)} %copy.20, s32[1024]{0:T(1024)S(1)} %get-tuple-element.13), kind=kCustom, calls=%fused_computation.clone | custom fusion | bytes 18874404 | tf_op jit(solution)/shard_map/jit(_take)/gather | solution.py:21
  322.9 0.0 copy-start.1
  322.9 10.0 %fusion = f32[9,128,128]{2,1,0:T(8,128)} fusion(bf16[9,128,4096]{2,1,0:T(8,128)(2,1)} %gather_fusion.2, bf16[9,128,4096]{2,1,0:T(8,128)(2,1)} %gather_fusion.1, pred[9]{0:T(512)(128)(4,1)S(1)} %get-tuple-element.10, pred[9]{0:T(512)(128)(4,1)S(1)} %get-tuple-element.6), kind=kOutput, calls=%fused_computation.3 | convolution fusion | flops 1217396736 | bytes 19464210 | tf_op jit(solution)/shard_map/sbw,scw->sbc/dot_general | solution.py:23
  332.9 0.0 all-gather.6.cloned.1.call-update
  332.9 39.3 %all-gather.6.cloned.1.call-done = f32[72,128,128]{2,1,0:T(8,128)} async-done(((f32[9,128,128]{2,1,0:T(8,128)}), f32[72,128,128]{2,1,0:T(8,128)}) %all-gather.6.cloned.1.call-update) | async-done | bytes 4718608 | tf_op jit(solution)/shard_map/all_gather | solution.py:26
  372.3 2.7 reduce_sum.9
  374.9 0.6 constant_dynamic-slice_fusion
  375.6 0.0 copy-done.1
  (4 shorter events, 0.1 us)
Async XLA Ops:
  6.5 0.9 copy-start
  6.5 258.2 %all-gather.4.cloned.1.call-start = ((), (), s32[]{:S(2)}) async-start(), calls=%async_computation | async-start | bytes 25559040 | tf_op jit(solution)/shard_map/all_gather | solution.py:20
  8.4 7.0 %copy-start.2 = (s32[9]{0:T(128)S(1)}, s32[9]{0:T(128)}, u32[]{:S(2)}) copy-start(s32[9]{0:T(128)} %param.9) | copy-start | bytes 112
  15.3 356.9 %all-gather.6.cloned.1.call-start = ((), (), s32[]{:S(2)}) async-start(), calls=%async_computation.1 | async-start | bytes 5308416 | tf_op jit(solution)/shard_map/all_gather | solution.py:26
  322.9 52.7 %copy-start.1 = (bf16[3072,32]{0,1:T(8,128)(2,1)S(1)}, bf16[3072,32]{0,1:T(8,128)(2,1)}, u32[]{:S(2)}) copy-start(bf16[3072,32]{0,1:T(8,128)(2,1)} %param.8) | copy-start | bytes 589828
Sparse Core Ops, SparseCore 0:
  15.4 249.3 all-gather.3
  333.0 39.1 all-gather.5

commit v2 on v0

--- a/solution.py
+++ b/solution.py
@@ -17,7 +17,9 @@
     halves = halves.reshape(block_count, tile_width, aux_count * local_occ)
     row_blocks = pair_owner // block_count
     col_blocks = pair_owner % block_count
-    gathered = lax.all_gather(halves, "aux", axis=2, tiled=True)
+    gathered = jnp.concatenate(
+        lax.all_to_all(jnp.stack([halves] * lax.axis_size("aux")), "aux", 0, 0), axis=2
+    )
     row_part = jnp.take(gathered, row_blocks, axis=0)
     col_part = jnp.take(gathered, col_blocks, axis=0)
     partial_tiles = jnp.einsum(

time: 415 us -> 1300 us (3.13)
  waiting for transfers between devices: 322 us -> 1190 us
  starting transfers between devices: 0.04 us -> 19.1 us
    all_to_all x0 -> x1, waiting for transfers between devices: none -> 1080 us  [shards(): lax.all_to_all(jnp.stack([halves] * lax.axis_size('aux')), 'aux', 0, 0)]
    all_gather x1 -> x0, waiting for transfers between devices: 248 us -> none  [shards(): gathered = lax.all_gather(halves, 'aux', axis=2, tiled=True)]
    psum x1, waiting for transfers between devices: 74.3 us -> 117 us  [shards(): summed = lax.psum(partial_tiles, 'occ')]
    all_gather x1 -> x0, local copies, waits for them, and re-layouts: 31.6 us -> none  [shards(): gathered = lax.all_gather(halves, 'aux', axis=2, tiled=True)]
    all_to_all x0 -> x1, local copies, waits for them, and re-layouts: none -> 20.9 us  [shards(): lax.all_to_all(jnp.stack([halves] * lax.axis_size('aux')), 'aux', 0, 0)]
    all_to_all x0 -> x1, starting transfers between devices: none -> 19 us  [shards(): lax.all_to_all(jnp.stack([halves] * lax.axis_size('aux')), 'aux', 0, 0)]
where the time goes in v2:
time: 1300 us
  waiting for transfers between devices  1190 us (92%)
  local copies, waits for them, and re-layouts  60 us (5%)
  starting transfers between devices  19.1 us (1%)
  matrix products  15.6 us (1%)
  between operations  13.5 us (1%)
    all_to_all x1, waiting for transfers between devices, shards(): lax.all_to_all(jnp.stack([halves] * lax.axis_size('aux')), 'aux', 0, 0)  1080 us
    psum x1, waiting for transfers between devices, shards(): summed = lax.psum(partial_tiles, 'occ')  117 us
  transfers between devices with their start and end apart: 2, of which 2 were waited for; matrix products, arithmetic and copies ran while one was open for 0% of the time, Pallas kernels for 0%

profile of v2, /device:TPU:8, one launch (start us, length us, event | category | flops | bytes accessed | tf_op | source)
XLA Modules:
  0.0 1301.5 jit_solution(2547052179520012658)
XLA Ops:
  6.5 0.0 copy-start
  6.5 0.9 copy-done
  7.5 0.7 compare_select_fusion
  8.2 0.1 copy.18
  8.3 0.1 reshape.37
  8.4 0.9 gather_fusion
  9.3 5.0 fusion.14
  14.3 9.1 stack.3
  23.4 0.0 copy-start.2
  23.4 19.0 %all-to-all-start = ((bf16[64,24,128,64]{2,3,1,0:T(8,128)(2,1)}), bf16[64,24,128,64]{2,3,1,0:T(8,128)(2,1)}, u32[]{:S(2)}, u32[]{:S(2)}) async-start(bf16[64,24,128,64]{2,3,1,0:T(8,128)(2,1)} %stack.3), calls=%async_computation | async-start | bytes 50331648 | tf_op jit(solution)/shard_map/all_to_all | solution.py:21
  42.4 0.0 all-reduce.2.cloned.1.call-start
  42.5 0.0 copy-done.2
  42.5 1075.6 %all-to-all-done = bf16[64,24,128,64]{2,3,1,0:T(8,128)(2,1)} async-done(((bf16[64,24,128,64]{2,3,1,0:T(8,128)(2,1)}), bf16[64,24,128,64]{2,3,1,0:T(8,128)(2,1)}, u32[]{:S(2)}, u32[]{:S(2)}) %all-to-all-start) | async-done | bytes 25165856 | tf_op jit(solution)/shard_map/all_to_all | solution.py:21
  1118.1 20.9 %copy.22 = bf16[64,24,128,64]{2,3,0,1:T(8,128)(2,1)} copy(bf16[64,24,128,64]{2,3,1,0:T(8,128)(2,1)} %all-to-all-done) | data formatting | bytes 50331648 | tf_op jit(solution)/shard_map/all_to_all | solution.py:21
  1138.9 13.2 %gather_fusion.2 = bf16[9,128,4096]{1,2,0:T(8,128)(2,1)} fusion(bf16[24,128,4096]{1,2,0:T(8,128)(2,1)} %bitcast.17, s32[1024]{0:T(1024)S(1)} %get-tuple-element.12), kind=kCustom, calls=%fused_computation.1.clone | custom fusion | bytes 18874404 | tf_op jit(solution)/shard_map/jit(_take)/gather | solution.py:24
  1152.1 13.3 %gather_fusion.1 = bf16[9,128,4096]{1,2,0:T(8,128)(2,1)} fusion(bf16[24,128,4096]{1,2,0:T(8,128)(2,1)} %bitcast.18, s32[1024]{0:T(1024)S(1)} %get-tuple-element.13), kind=kCustom, calls=%fused_computation.clone | custom fusion | bytes 18874404 | tf_op jit(solution)/shard_map/jit(_take)/gather | solution.py:23
  1165.3 0.0 copy-start.1
  1165.3 10.7 fusion
  1176.0 0.0 all-reduce.2.cloned.1.call-update
  1176.1 117.1 %all-reduce.2.cloned.1.call-done = f32[9,128,128]{2,1,0:T(8,128)} async-done(((f32[9,128,128]{2,1,0:T(8,128)}), f32[9,128,128]{2,1,0:T(8,128)}) %all-reduce.2.cloned.1.call-update) | async-done | bytes 589840 | tf_op jit(solution)/shard_map/psum | solution.py:28
  1293.2 1.5 constant_dynamic-slice_fusion
  1294.7 0.0 copy-done.1
  (4 shorter events, 0.1 us)
Async XLA Ops:
  6.5 0.9 copy-start
  23.4 19.1 %copy-start.2 = (s32[9]{0:T(128)S(1)}, s32[9]{0:T(128)}, u32[]{:S(2)}) copy-start(s32[9]{0:T(128)} %param.9) | copy-start | bytes 112
  23.4 1094.7 %all-to-all-start = ((bf16[64,24,128,64]{2,3,1,0:T(8,128)(2,1)}), bf16[64,24,128,64]{2,3,1,0:T(8,128)(2,1)}, u32[]{:S(2)}, u32[]{:S(2)}) async-start(bf16[64,24,128,64]{2,3,1,0:T(8,128)(2,1)} %stack.3), calls=%async_computation | async-start | bytes 50331648 | tf_op jit(solution)/shard_map/all_to_all | solution.py:21
  42.4 1250.8 %all-reduce.2.cloned.1.call-start = ((), (), s32[]{:S(2)}) async-start(), calls=%async_computation.1 | async-start | bytes 1179648 | tf_op jit(solution)/shard_map/psum | solution.py:28
  1165.3 129.3 %copy-start.1 = (bf16[3072,32]{0,1:T(8,128)(2,1)S(1)}, bf16[3072,32]{0,1:T(8,128)(2,1)}, u32[]{:S(2)}) copy-start(bf16[3072,32]{0,1:T(8,128)(2,1)} %param.8) | copy-start | bytes 589828
Sparse Core Ops, SparseCore 0:
  1176.2 116.9 all-reduce.1
